TPU v7x, 512 devices: a whole 4x8x8 slice. The times are simulated.
512 devices in a mesh: ctxa: 16 (over z, core), ctxb: 32 (over x, y).
Axes of the slice: x: 4, y: 8, z: 8, core: 2. Of those that a mesh axis runs over, the one named last changes fastest.
Arguments:
- queries: bfloat16 [131072, 8, 128], P(('ctxa', 'ctxb')), may hold values from -14 to 14
- key_vectors: bfloat16 [131072, 128], P(('ctxa', 'ctxb')), may hold values from -5 to 5
- value_vectors: bfloat16 [131072, 128], P(('ctxa', 'ctxb')), may hold values from -12 to 12
- out_grad: bfloat16 [131072, 8, 128], P(('ctxa', 'ctxb')), may hold values from -6 to 6
Outputs:
- attention: bfloat16 [131072, 8, 128], P(('ctxa', 'ctxb'))
- query_grad: bfloat16 [131072, 8, 128], P(('ctxa', 'ctxb'))
- key_grad: bfloat16 [131072, 128], P(('ctxa', 'ctxb'))
- value_grad: bfloat16 [131072, 128], P(('ctxa', 'ctxb'))
All inputs are finite; a program needn't handle non-finite values.
Results may differ from a plain program's by a relative error of at most 0.012.
Values may be sent and summed in bfloat16 or wider, within the bound.
A program may use at most 64 MiB of HBM per device.

v0:
```python
import jax
import jax.numpy as jnp
from jax import lax
from jax.sharding import PartitionSpec as P

BLK = 128
WIN = 1024
FAR = 6


def shifted(value, axis, by):
    count = lax.axis_size(axis)
    pairs = [(i, i + by) for i in range(count) if 0 <= i + by < count]
    return lax.ppermute(value, axis, pairs)


def body(queries, key_vectors, value_vectors, out_grad):
    tok_count = key_vectors.shape[0]
    heads = queries.shape[1]
    width = key_vectors.shape[1]
    score_scale = 1.0 / width**0.5
    inner_size = lax.axis_size("ctxb")
    devices_all = lax.axis_size("ctxa") * inner_size
    device = lax.axis_index("ctxa") * inner_size + lax.axis_index("ctxb")
    start_pos = device * tok_count
    shards = WIN // tok_count
    stride = 2 * WIN // BLK
    half_block = BLK // 2
    key_span = WIN + BLK
    paired = jnp.stack([key_vectors, value_vectors])
    steps_done = []
    held_pairs = paired
    held_count = 1
    while held_count < shards + 1:
        take_count = min(held_count, shards + 1 - held_count)
        moved = shifted(
            held_pairs[:, (held_count - take_count) * tok_count :], ("ctxa", "ctxb"), held_count
        )
        steps_done.append((held_count, take_count))
        held_pairs = jnp.concatenate([moved, held_pairs], axis=1)
        held_count = held_count + take_count
    window_pairs = held_pairs
    distances = []
    far_list = []
    for level_index in range(FAR):
        distance = stride * 2**level_index * BLK // tok_count
        far_list.append(shifted(paired, ("ctxa", "ctxb"), distance))
        distances.append(distance)
    level_count = len(distances)
    far_pairs = jnp.stack(far_list, axis=1)
    far_valid = jnp.stack([device >= distance for distance in distances])
    far_keys = level_count * BLK
    total_keys = key_span + far_keys
    offsets = jnp.arange(key_span, dtype=jnp.int32)
    inside = jnp.arange(half_block, dtype=jnp.int32)
    far_mask = jnp.broadcast_to(jnp.repeat(far_valid, BLK)[None, :], (half_block, far_keys))
    row_count = half_block * heads

    def sub_block(block_index, running):
        attention, query_grad, window_grad, far_grad = running
        first_row = block_index * half_block
        key_start = first_row // BLK * BLK
        window_part = lax.dynamic_slice_in_dim(window_pairs, key_start, key_span, 1)
        far_part = lax.dynamic_slice_in_dim(far_pairs, key_start, BLK, 2).reshape(
            2, far_keys, width
        )
        key_rows = jnp.concatenate([window_part[0], far_part[0]], axis=0)
        value_rows = jnp.concatenate([window_part[1], far_part[1]], axis=0)
        q_pos = start_pos + first_row + inside
        k_pos = start_pos - WIN + key_start + offsets
        near_mask = (
            (k_pos[None, :] > q_pos[:, None] - WIN)
            & (k_pos[None, :] <= q_pos[:, None])
            & (k_pos[None, :] >= 0)
        )
        visible = jnp.concatenate([near_mask, far_mask], axis=1)
        visible = jnp.broadcast_to(visible[:, None, :], (half_block, heads, total_keys)).reshape(
            row_count, total_keys
        )
        q_rows = lax.dynamic_slice_in_dim(queries, first_row, half_block, 0).reshape(
            row_count, width
        )
        grad_rows = lax.dynamic_slice_in_dim(out_grad, first_row, half_block, 0).reshape(
            row_count, width
        )
        scores = (
            jnp.einsum("rd,kd->rk", q_rows, key_rows, preferred_element_type=jnp.float32)
            * score_scale
        )
        scores = jnp.where(visible, scores, -jnp.inf)
        row_max = jnp.max(scores, axis=1, keepdims=True)
        log_total = row_max + jnp.log(jnp.sum(jnp.exp(scores - row_max), axis=1, keepdims=True))
        probs = jnp.exp(scores - log_total)
        probs_low = probs.astype(jnp.bfloat16)
        out_rows = jnp.dot(probs_low, value_rows, preferred_element_type=jnp.float32).astype(
            jnp.bfloat16
        )
        row_delta = jnp.sum(
            grad_rows.astype(jnp.float32) * out_rows.astype(jnp.float32), axis=1, keepdims=True
        )
        prob_grad = jnp.einsum(
            "rd,kd->rk", grad_rows, value_rows, preferred_element_type=jnp.float32
        )
        score_grad = (probs * (prob_grad - row_delta)).astype(jnp.bfloat16)
        q_grad_rows = (
            jnp.dot(score_grad, key_rows, preferred_element_type=jnp.float32) * score_scale
        ).astype(jnp.bfloat16)
        key_terms = (
            jnp.einsum("rk,rd->kd", score_grad, q_rows, preferred_element_type=jnp.float32)
            * score_scale
        )
        value_terms = jnp.einsum(
            "rk,rd->kd", probs_low, grad_rows, preferred_element_type=jnp.float32
        )
        grad_terms = jnp.stack([key_terms, value_terms])
        previous = lax.dynamic_slice_in_dim(window_grad, key_start, key_span, 1)
        window_grad = lax.dynamic_update_slice_in_dim(
            window_grad, previous + grad_terms[:, :key_span], key_start, 1
        )
        far_terms = grad_terms[:, key_span:].reshape(2, level_count, BLK, width)
        previous_far = lax.dynamic_slice_in_dim(far_grad, key_start, BLK, 2)
        far_grad = lax.dynamic_update_slice_in_dim(far_grad, previous_far + far_terms, key_start, 2)
        attention = lax.dynamic_update_slice_in_dim(
            attention, out_rows.reshape(half_block, heads, width), first_row, 0
        )
        query_grad = lax.dynamic_update_slice_in_dim(
            query_grad, q_grad_rows.reshape(half_block, heads, width), first_row, 0
        )
        return (attention, query_grad, window_grad, far_grad)

    running = (
        jnp.zeros((tok_count, heads, width), jnp.bfloat16),
        jnp.zeros((tok_count, heads, width), jnp.bfloat16),
        jnp.zeros((2, WIN + tok_count, width), jnp.float32),
        jnp.zeros((2, level_count, tok_count, width), jnp.float32),
    )
    attention, query_grad, window_grad, far_grad = lax.fori_loop(
        0, tok_count // half_block, sub_block, running
    )
    grad_held = window_grad
    for held_count, take_count in reversed(steps_done):
        returned = shifted(grad_held[:, : take_count * tok_count], ("ctxa", "ctxb"), -held_count)
        grad_held = grad_held[:, take_count * tok_count :]
        grad_held = jnp.concatenate(
            [
                grad_held[:, : (held_count - take_count) * tok_count],
                grad_held[:, (held_count - take_count) * tok_count :] + returned,
            ],
            axis=1,
        )
    own_grad = grad_held
    for level_index, distance in enumerate(distances):
        own_grad = own_grad + shifted(far_grad[:, level_index], ("ctxa", "ctxb"), -distance)
    return (
        attention,
        query_grad,
        own_grad[0].astype(jnp.bfloat16),
        own_grad[1].astype(jnp.bfloat16),
    )


def solution(mesh):
    in_specs = (
        P(("ctxa", "ctxb"), None, None),
        P(("ctxa", "ctxb"), None),
        P(("ctxa", "ctxb"), None),
        P(("ctxa", "ctxb"), None, None),
    )
    out_specs = (
        P(("ctxa", "ctxb"), None, None),
        P(("ctxa", "ctxb"), None, None),
        P(("ctxa", "ctxb"), None),
        P(("ctxa", "ctxb"), None),
    )
    return jax.shard_map(body, mesh=mesh, in_specs=in_specs, out_specs=out_specs, check_vma=False)
```

profile of v0, /device:TPU:121, one launch (start us, length us, event | category | flops | bytes accessed | tf_op | source)
XLA Modules:
  0.0 181.6 jit_solution(16202441559973571689)
XLA Ops:
  0.7 0.9 pad_maximum_fusion.8
  1.6 2.3 %collective-permute-start.1 = (bf16[2,256,128]{2,1,0:T(8,128)(2,1)S(1)}, bf16[2,256,128]{2,1,0:T(8,128)(2,1)S(1)}, u32[]{:S(2)}, u32[]{:S(2)}) collective-permute-start(bf16[2,256,128]{2,1,0:T(8,128)(2,1)S(1)} %pad_maximum_fusion.8), channel_id=1, source_target_pairs={{0,1},{1,2},{2,3},{3,4},{4,5},{5,6},{6,7},{7,8},{8,9},{9,10},{10,1... | collective-permute-start | bytes 393224 | tf_op jit(solution)/shard_map/ppermute | solution.py:14
  3.9 7.5 %collective-permute-start = (bf16[2,256,128]{2,1,0:T(8,128)(2,1)S(1)}, bf16[2,256,128]{2,1,0:T(8,128)(2,1)S(1)}, u32[]{:S(2)}, u32[]{:S(2)}) collective-permute-start(bf16[2,256,128]{2,1,0:T(8,128)(2,1)S(1)} %pad_maximum_fusion.8), channel_id=1, source_target_pairs={{0,4},{1,5},{2,6},{3,7},{4,8},{5,9},{6,10},{7,11},{8,12},{9,13},{1... | collective-permute-start | bytes 393224 | tf_op jit(solution)/shard_map/ppermute | solution.py:14
  11.4 3.1 %collective-permute-start.3 = (bf16[2,256,128]{2,1,0:T(8,128)(2,1)S(1)}, bf16[2,256,128]{2,1,0:T(8,128)(2,1)S(1)}, u32[]{:S(2)}, u32[]{:S(2)}) collective-permute-start(bf16[2,256,128]{2,1,0:T(8,128)(2,1)S(1)} %pad_maximum_fusion.8), channel_id=1, source_target_pairs={{0,8},{1,9},{2,10},{3,11},{4,12},{5,13},{6,14},{7,15},{8,16},{9,17... | collective-permute-start | bytes 393224 | tf_op jit(solution)/shard_map/ppermute | solution.py:14
  14.5 6.0 %collective-permute-start.4 = (bf16[2,256,128]{2,1,0:T(8,128)(2,1)S(1)}, bf16[2,256,128]{2,1,0:T(8,128)(2,1)S(1)}, u32[]{:S(2)}, u32[]{:S(2)}) collective-permute-start(bf16[2,256,128]{2,1,0:T(8,128)(2,1)S(1)} %pad_maximum_fusion.8), channel_id=1, source_target_pairs={{0,16},{1,17},{2,18},{3,19},{4,20},{5,21},{6,22},{7,23},{8,24},{9,... | collective-permute-start | bytes 393224 | tf_op jit(solution)/shard_map/ppermute | solution.py:14
  20.5 2.6 %collective-permute-start.5 = (bf16[2,256,128]{2,1,0:T(8,128)(2,1)S(1)}, bf16[2,256,128]{2,1,0:T(8,128)(2,1)S(1)}, u32[]{:S(2)}, u32[]{:S(2)}) collective-permute-start(bf16[2,256,128]{2,1,0:T(8,128)(2,1)S(1)} %pad_maximum_fusion.8), channel_id=1, source_target_pairs={{0,32},{1,33},{2,34},{3,35},{4,36},{5,37},{6,38},{7,39},{8,40},{9,... | collective-permute-start | bytes 393224 | tf_op jit(solution)/shard_map/ppermute | solution.py:14
  23.3 4.0 %collective-permute-start.6 = (bf16[2,256,128]{2,1,0:T(8,128)(2,1)S(1)}, bf16[2,256,128]{2,1,0:T(8,128)(2,1)S(1)}, u32[]{:S(2)}, u32[]{:S(2)}) collective-permute-start(bf16[2,256,128]{2,1,0:T(8,128)(2,1)S(1)} %pad_maximum_fusion.8), channel_id=1, source_target_pairs={{0,64},{1,65},{2,66},{3,67},{4,68},{5,69},{6,70},{7,71},{8,72},{9,... | collective-permute-start | bytes 393224 | tf_op jit(solution)/shard_map/ppermute | solution.py:14
  27.3 6.1 %collective-permute-start.7 = (bf16[2,256,128]{2,1,0:T(8,128)(2,1)S(1)}, bf16[2,256,128]{2,1,0:T(8,128)(2,1)S(1)}, u32[]{:S(2)}, u32[]{:S(2)}) collective-permute-start(bf16[2,256,128]{2,1,0:T(8,128)(2,1)S(1)} %pad_maximum_fusion.8), channel_id=1, source_target_pairs={{0,128},{1,129},{2,130},{3,131},{4,132},{5,133},{6,134},{7,135},{8... | collective-permute-start | bytes 393224 | tf_op jit(solution)/shard_map/ppermute | solution.py:14
  33.5 3.7 %collective-permute-start.8 = (bf16[2,256,128]{2,1,0:T(8,128)(2,1)S(1)}, bf16[2,256,128]{2,1,0:T(8,128)(2,1)S(1)}, u32[]{:S(2)}, u32[]{:S(2)}) collective-permute-start(bf16[2,256,128]{2,1,0:T(8,128)(2,1)S(1)} %pad_maximum_fusion.8), channel_id=1, source_target_pairs={{0,256},{1,257},{2,258},{3,259},{4,260},{5,261},{6,262},{7,263},{8... | collective-permute-start | bytes 393224 | tf_op jit(solution)/shard_map/ppermute | solution.py:14
  37.2 0.9 maximum_maximum_fusion.1
  38.1 1.9 %collective-permute-start.2 = (bf16[2,512,128]{2,1,0:T(8,128)(2,1)S(1)}, bf16[2,512,128]{2,1,0:T(8,128)(2,1)S(1)}, u32[]{:S(2)}, u32[]{:S(2)}) collective-permute-start(bf16[2,512,128]{2,1,0:T(8,128)(2,1)S(1)} %maximum_maximum_fusion.1), channel_id=1, source_target_pairs={{0,2},{1,3},{2,4},{3,5},{4,6},{5,7},{6,8},{7,9},{8,10},{9,11},{10,... | collective-permute-start | bytes 786440 | tf_op jit(solution)/shard_map/ppermute | solution.py:14
  40.1 2.0 %collective-permute-done.7 = bf16[2,256,128]{2,1,0:T(8,128)(2,1)S(1)} collective-permute-done((bf16[2,256,128]{2,1,0:T(8,128)(2,1)S(1)}, bf16[2,256,128]{2,1,0:T(8,128)(2,1)S(1)}, u32[]{:S(2)}, u32[]{:S(2)}) %collective-permute-start.7) | collective-permute-done | bytes 131104 | tf_op jit(solution)/shard_map/ppermute | solution.py:14
  42.6 7.6 %collective-permute-done.2 = bf16[2,512,128]{2,1,0:T(8,128)(2,1)S(1)} collective-permute-done((bf16[2,512,128]{2,1,0:T(8,128)(2,1)S(1)}, bf16[2,512,128]{2,1,0:T(8,128)(2,1)S(1)}, u32[]{:S(2)}, u32[]{:S(2)}) %collective-permute-start.2) | collective-permute-done | bytes 262176 | tf_op jit(solution)/shard_map/ppermute | solution.py:14
  50.2 0.9 maximum_maximum_fusion
  51.1 0.9 broadcast.109
  52.0 0.9 broadcast.109.clone
  53.1 55.3 %while.23 = (s32[]{:T(128)}, bf16[256,8,128]{2,1,0:T(8,128)(2,1)}, bf16[256,8,128]{2,1,0:T(8,128)(2,1)}, f32[2,1280,128]{2,1,0:T(8,128)S(1)}, f32[2,6,256,128]{3...) while((s32[]{:T(128)}, bf16[256,8,128]{2,1,0:T(8,128)(2,1)}, ...), condition=%wide.region_4.5_spmd.clone, body=%wide.region_0.4_spmd.clone.sunk | while | flops 1528769024 | bytes 46571916 | solution.py:137
  53.1 1.8 constant_dynamic-slice_fusion.8
  54.9 1.8 dynamic-slice_bitcast_fusion.3
  57.0 2.3 %fusion.59 = (f32[512]{0:T(512)S(1)}, f32[512,1920]{1,0:T(8,128)S(1)}) fusion(bf16[768,128]{1,0:T(8,128)(2,1)} %bitcast.115, bf16[1152,128]{1,0:T(8,128)(2,1)} %get-tuple-element.522, bf16[256,8,128]{2,1,0:T(8,128)(2,1)} %get-tuple-element.582, s32[]{:T(128)S(6)} %select_n.75, pred[64,1920]{1,0:T(8,128)(4,1)S(1)} %pad_add_fusion.2), kind=kOutput, calls=%fused_computation.85.clone.1 | convolution fusion | flops 255589888 | bytes 4679684 | tf_op jit(solution)/shard_map/while/body/eval_jaxpr/rd,kd->rk/dot_general | solution.py:87
  59.2 0.7 exponential_reduce_fusion.2
  59.9 1.4 bitcast_dynamic-update-slice_fusion.8
  61.5 1.0 multiply_convert_fusion.2
  62.6 1.3 fusion.60
  63.9 1.6 fusion.61
  65.5 0.9 convolution_bitcast_fusion.2
  67.0 1.8 constant_dynamic-slice_fusion.8
  68.7 1.8 dynamic-slice_bitcast_fusion.3
  70.8 2.3 %fusion.59 = (f32[512]{0:T(512)S(1)}, f32[512,1920]{1,0:T(8,128)S(1)}) fusion(bf16[768,128]{1,0:T(8,128)(2,1)} %bitcast.115, bf16[1152,128]{1,0:T(8,128)(2,1)} %get-tuple-element.522, bf16[256,8,128]{2,1,0:T(8,128)(2,1)} %get-tuple-element.582, s32[]{:T(128)S(6)} %select_n.75, pred[64,1920]{1,0:T(8,128)(4,1)S(1)} %pad_add_fusion.2), kind=kOutput, calls=%fused_computation.85.clone.1 | convolution fusion | flops 255589888 | bytes 4679684 | tf_op jit(solution)/shard_map/while/body/eval_jaxpr/rd,kd->rk/dot_general | solution.py:87
  73.0 0.7 exponential_reduce_fusion.2
  73.7 1.4 bitcast_dynamic-update-slice_fusion.8
  75.3 1.0 multiply_convert_fusion.2
  76.4 1.3 fusion.60
  77.7 1.6 fusion.61
  79.4 0.9 convolution_bitcast_fusion.2
  80.8 1.8 constant_dynamic-slice_fusion.8
  82.6 1.8 dynamic-slice_bitcast_fusion.3
  84.6 2.3 %fusion.59 = (f32[512]{0:T(512)S(1)}, f32[512,1920]{1,0:T(8,128)S(1)}) fusion(bf16[768,128]{1,0:T(8,128)(2,1)} %bitcast.115, bf16[1152,128]{1,0:T(8,128)(2,1)} %get-tuple-element.522, bf16[256,8,128]{2,1,0:T(8,128)(2,1)} %get-tuple-element.582, s32[]{:T(128)S(6)} %select_n.75, pred[64,1920]{1,0:T(8,128)(4,1)S(1)} %pad_add_fusion.2), kind=kOutput, calls=%fused_computation.85.clone.1 | convolution fusion | flops 255589888 | bytes 4679684 | tf_op jit(solution)/shard_map/while/body/eval_jaxpr/rd,kd->rk/dot_general | solution.py:87
  86.9 0.7 exponential_reduce_fusion.2
  87.6 1.4 bitcast_dynamic-update-slice_fusion.8
  89.2 1.0 multiply_convert_fusion.2
  90.2 1.3 fusion.60
  91.6 1.6 fusion.61
  93.2 0.9 convolution_bitcast_fusion.2
  94.6 1.8 constant_dynamic-slice_fusion.8
  96.4 1.8 dynamic-slice_bitcast_fusion.3
  98.5 2.3 %fusion.59 = (f32[512]{0:T(512)S(1)}, f32[512,1920]{1,0:T(8,128)S(1)}) fusion(bf16[768,128]{1,0:T(8,128)(2,1)} %bitcast.115, bf16[1152,128]{1,0:T(8,128)(2,1)} %get-tuple-element.522, bf16[256,8,128]{2,1,0:T(8,128)(2,1)} %get-tuple-element.582, s32[]{:T(128)S(6)} %select_n.75, pred[64,1920]{1,0:T(8,128)(4,1)S(1)} %pad_add_fusion.2), kind=kOutput, calls=%fused_computation.85.clone.1 | convolution fusion | flops 255589888 | bytes 4679684 | tf_op jit(solution)/shard_map/while/body/eval_jaxpr/rd,kd->rk/dot_general | solution.py:87
  100.7 0.7 exponential_reduce_fusion.2
  101.4 1.4 bitcast_dynamic-update-slice_fusion.8
  103.0 1.0 multiply_convert_fusion.2
  104.1 1.3 fusion.60
  105.4 1.6 fusion.61
  107.0 0.9 convolution_bitcast_fusion.2
  108.5 2.2 %collective-permute-start.10 = (f32[2,512,128]{2,1,0:T(8,128)S(1)}, f32[2,512,128]{2,1,0:T(8,128)S(1)}, u32[]{:S(2)}, u32[]{:S(2)}) collective-permute-start(f32[2,512,128]{2,1,0:T(8,128)S(1)} %slice.123), channel_id=1, source_target_pairs={{2,0},{3,1},{4,2},{5,3},{6,4},{7,5},{8,6},{9,7},{10,8},{11,9},{12,... | collective-permute-start | bytes 1572872 | tf_op jit(solution)/shard_map/ppermute | solution.py:14
  110.8 11.3 %collective-permute-start.9 = (f32[2,256,128]{2,1,0:T(8,128)S(1)}, f32[2,256,128]{2,1,0:T(8,128)S(1)}, u32[]{:S(2)}, u32[]{:S(2)}) collective-permute-start(f32[2,256,128]{2,1,0:T(8,128)S(1)} %slice.121), channel_id=1, source_target_pairs={{4,0},{5,1},{6,2},{7,3},{8,4},{9,5},{10,6},{11,7},{12,8},{13,9},{1... | collective-permute-start | bytes 786440 | tf_op jit(solution)/shard_map/ppermute | solution.py:14
  122.2 1.3 collective-permute-start.17
  123.5 1.3 collective-permute-start.16
  124.8 3.4 %collective-permute-start.15 = (f32[2,256,128]{2,1,0:T(8,128)S(1)}, f32[2,256,128]{2,1,0:T(8,128)S(1)}, u32[]{:S(2)}, u32[]{:S(2)}) collective-permute-start(f32[2,256,128]{2,1,0:T(8,128)S(1)} %get-tuple-element.430), channel_id=1, source_target_pairs={{64,0},{65,1},{66,2},{67,3},{68,4},{69,5},{70,6},{71,7},{72,8},{73... | collective-permute-start | bytes 786440 | tf_op jit(solution)/shard_map/ppermute | solution.py:14
  128.2 18.4 %collective-permute-done.9 = f32[2,256,128]{2,1,0:T(8,128)S(1)} collective-permute-done((f32[2,256,128]{2,1,0:T(8,128)S(1)}, f32[2,256,128]{2,1,0:T(8,128)S(1)}, u32[]{:S(2)}, u32[]{:S(2)}) %collective-permute-start.9) | collective-permute-done | bytes 262176 | tf_op jit(solution)/shard_map/ppermute | solution.py:14
  146.6 2.9 %collective-permute-start.14 = (f32[2,256,128]{2,1,0:T(8,128)S(1)}, f32[2,256,128]{2,1,0:T(8,128)S(1)}, u32[]{:S(2)}, u32[]{:S(2)}) collective-permute-start(f32[2,256,128]{2,1,0:T(8,128)S(1)} %get-tuple-element.431), channel_id=1, source_target_pairs={{32,0},{33,1},{34,2},{35,3},{36,4},{37,5},{38,6},{39,7},{40,8},{41... | collective-permute-start | bytes 786440 | tf_op jit(solution)/shard_map/ppermute | solution.py:14
  149.5 2.6 %collective-permute-start.13 = (f32[2,256,128]{2,1,0:T(8,128)S(1)}, f32[2,256,128]{2,1,0:T(8,128)S(1)}, u32[]{:S(2)}, u32[]{:S(2)}) collective-permute-start(f32[2,256,128]{2,1,0:T(8,128)S(1)} %get-tuple-element.432), channel_id=1, source_target_pairs={{16,0},{17,1},{18,2},{19,3},{20,4},{21,5},{22,6},{23,7},{24,8},{25... | collective-permute-start | bytes 786440 | tf_op jit(solution)/shard_map/ppermute | solution.py:14
  152.2 13.3 %collective-permute-start.12 = (f32[2,256,128]{2,1,0:T(8,128)S(1)}, f32[2,256,128]{2,1,0:T(8,128)S(1)}, u32[]{:S(2)}, u32[]{:S(2)}) collective-permute-start(f32[2,256,128]{2,1,0:T(8,128)S(1)} %get-tuple-element.428), channel_id=1, source_target_pairs={{8,0},{9,1},{10,2},{11,3},{12,4},{13,5},{14,6},{15,7},{16,8},{17,9... | collective-permute-start | bytes 786440 | tf_op jit(solution)/shard_map/ppermute | solution.py:14
  165.5 1.9 %collective-permute-start.11 = (f32[2,256,128]{2,1,0:T(8,128)S(1)}, f32[2,256,128]{2,1,0:T(8,128)S(1)}, u32[]{:S(2)}, u32[]{:S(2)}) collective-permute-start(f32[2,256,128]{2,1,0:T(8,128)S(1)} %slice.143), channel_id=1, source_target_pairs={{1,0},{2,1},{3,2},{4,3},{5,4},{6,5},{7,6},{8,7},{9,8},{10,9},{11,1... | collective-permute-start | bytes 786440 | tf_op jit(solution)/shard_map/ppermute | solution.py:14
  167.4 13.4 %collective-permute-done.12 = f32[2,256,128]{2,1,0:T(8,128)S(1)} collective-permute-done((f32[2,256,128]{2,1,0:T(8,128)S(1)}, f32[2,256,128]{2,1,0:T(8,128)S(1)}, u32[]{:S(2)}, u32[]{:S(2)}) %collective-permute-start.12) | collective-permute-done | bytes 262176 | tf_op jit(solution)/shard_map/ppermute | solution.py:14
  (107 shorter events, 5.4 us)
Async XLA Ops:
  0.6 49.6 %copy-start.4 = (bf16[256,128]{1,0:T(8,128)(2,1)S(1)}, bf16[256,128]{1,0:T(8,128)(2,1)}, u32[]{:S(2)}) copy-start(bf16[256,128]{1,0:T(8,128)(2,1)} %param.8) | copy-start | bytes 196612
  0.6 49.6 %copy-start.5 = (bf16[256,128]{1,0:T(8,128)(2,1)S(1)}, bf16[256,128]{1,0:T(8,128)(2,1)}, u32[]{:S(2)}) copy-start(bf16[256,128]{1,0:T(8,128)(2,1)} %param.7) | copy-start | bytes 196612
  1.6 31.9 %collective-permute-start.1 = (bf16[2,256,128]{2,1,0:T(8,128)(2,1)S(1)}, bf16[2,256,128]{2,1,0:T(8,128)(2,1)S(1)}, u32[]{:S(2)}, u32[]{:S(2)}) collective-permute-start(bf16[2,256,128]{2,1,0:T(8,128)(2,1)S(1)} %pad_maximum_fusion.8), channel_id=1, source_target_pairs={{0,1},{1,2},{2,3},{3,4},{4,5},{5,6},{6,7},{7,8},{8,9},{9,10},{10,1... | collective-permute-start | bytes 393224 | tf_op jit(solution)/shard_map/ppermute | solution.py:14
  3.9 38.7 %collective-permute-start = (bf16[2,256,128]{2,1,0:T(8,128)(2,1)S(1)}, bf16[2,256,128]{2,1,0:T(8,128)(2,1)S(1)}, u32[]{:S(2)}, u32[]{:S(2)}) collective-permute-start(bf16[2,256,128]{2,1,0:T(8,128)(2,1)S(1)} %pad_maximum_fusion.8), channel_id=1, source_target_pairs={{0,4},{1,5},{2,6},{3,7},{4,8},{5,9},{6,10},{7,11},{8,12},{9,13},{1... | collective-permute-start | bytes 393224 | tf_op jit(solution)/shard_map/ppermute | solution.py:14
  11.4 11.9 %collective-permute-start.3 = (bf16[2,256,128]{2,1,0:T(8,128)(2,1)S(1)}, bf16[2,256,128]{2,1,0:T(8,128)(2,1)S(1)}, u32[]{:S(2)}, u32[]{:S(2)}) collective-permute-start(bf16[2,256,128]{2,1,0:T(8,128)(2,1)S(1)} %pad_maximum_fusion.8), channel_id=1, source_target_pairs={{0,8},{1,9},{2,10},{3,11},{4,12},{5,13},{6,14},{7,15},{8,16},{9,17... | collective-permute-start | bytes 393224 | tf_op jit(solution)/shard_map/ppermute | solution.py:14
  14.5 12.8 %collective-permute-start.4 = (bf16[2,256,128]{2,1,0:T(8,128)(2,1)S(1)}, bf16[2,256,128]{2,1,0:T(8,128)(2,1)S(1)}, u32[]{:S(2)}, u32[]{:S(2)}) collective-permute-start(bf16[2,256,128]{2,1,0:T(8,128)(2,1)S(1)} %pad_maximum_fusion.8), channel_id=1, source_target_pairs={{0,16},{1,17},{2,18},{3,19},{4,20},{5,21},{6,22},{7,23},{8,24},{9,... | collective-permute-start | bytes 393224 | tf_op jit(solution)/shard_map/ppermute | solution.py:14
  20.5 17.6 %collective-permute-start.5 = (bf16[2,256,128]{2,1,0:T(8,128)(2,1)S(1)}, bf16[2,256,128]{2,1,0:T(8,128)(2,1)S(1)}, u32[]{:S(2)}, u32[]{:S(2)}) collective-permute-start(bf16[2,256,128]{2,1,0:T(8,128)(2,1)S(1)} %pad_maximum_fusion.8), channel_id=1, source_target_pairs={{0,32},{1,33},{2,34},{3,35},{4,36},{5,37},{6,38},{7,39},{8,40},{9,... | collective-permute-start | bytes 393224 | tf_op jit(solution)/shard_map/ppermute | solution.py:14
  23.3 16.8 %collective-permute-start.6 = (bf16[2,256,128]{2,1,0:T(8,128)(2,1)S(1)}, bf16[2,256,128]{2,1,0:T(8,128)(2,1)S(1)}, u32[]{:S(2)}, u32[]{:S(2)}) collective-permute-start(bf16[2,256,128]{2,1,0:T(8,128)(2,1)S(1)} %pad_maximum_fusion.8), channel_id=1, source_target_pairs={{0,64},{1,65},{2,66},{3,67},{4,68},{5,69},{6,70},{7,71},{8,72},{9,... | collective-permute-start | bytes 393224 | tf_op jit(solution)/shard_map/ppermute | solution.py:14
  27.3 14.8 %collective-permute-start.7 = (bf16[2,256,128]{2,1,0:T(8,128)(2,1)S(1)}, bf16[2,256,128]{2,1,0:T(8,128)(2,1)S(1)}, u32[]{:S(2)}, u32[]{:S(2)}) collective-permute-start(bf16[2,256,128]{2,1,0:T(8,128)(2,1)S(1)} %pad_maximum_fusion.8), channel_id=1, source_target_pairs={{0,128},{1,129},{2,130},{3,131},{4,132},{5,133},{6,134},{7,135},{8... | collective-permute-start | bytes 393224 | tf_op jit(solution)/shard_map/ppermute | solution.py:14
  33.5 9.1 %collective-permute-start.8 = (bf16[2,256,128]{2,1,0:T(8,128)(2,1)S(1)}, bf16[2,256,128]{2,1,0:T(8,128)(2,1)S(1)}, u32[]{:S(2)}, u32[]{:S(2)}) collective-permute-start(bf16[2,256,128]{2,1,0:T(8,128)(2,1)S(1)} %pad_maximum_fusion.8), channel_id=1, source_target_pairs={{0,256},{1,257},{2,258},{3,259},{4,260},{5,261},{6,262},{7,263},{8... | collective-permute-start | bytes 393224 | tf_op jit(solution)/shard_map/ppermute | solution.py:14
  38.1 12.1 %collective-permute-start.2 = (bf16[2,512,128]{2,1,0:T(8,128)(2,1)S(1)}, bf16[2,512,128]{2,1,0:T(8,128)(2,1)S(1)}, u32[]{:S(2)}, u32[]{:S(2)}) collective-permute-start(bf16[2,512,128]{2,1,0:T(8,128)(2,1)S(1)} %maximum_maximum_fusion.1), channel_id=1, source_target_pairs={{0,2},{1,3},{2,4},{3,5},{4,6},{5,7},{6,8},{7,9},{8,10},{9,11},{10,... | collective-permute-start | bytes 786440 | tf_op jit(solution)/shard_map/ppermute | solution.py:14
  42.6 9.4 %copy-start.3 = (bf16[2,6,256,128]{3,2,1,0:T(8,128)(2,1)}, bf16[2,6,256,128]{3,2,1,0:T(8,128)(2,1)S(1)}, u32[]{:S(2)}) copy-start(bf16[2,6,256,128]{3,2,1,0:T(8,128)(2,1)S(1)} %bitcast_dynamic-update-slice_fusion.6) | copy-start | bytes 2359300
  59.9 1.4 copy-start.2
  61.5 1.1 copy-start
  61.5 1.1 copy-start.1
  73.7 1.4 copy-start.2
  75.3 1.1 copy-start
  75.3 1.1 copy-start.1
  87.6 1.4 copy-start.2
  89.2 1.1 copy-start
  89.2 1.1 copy-start.1
  101.4 1.4 copy-start.2
  103.0 1.1 copy-start
  103.0 1.1 copy-start.1
  108.5 41.0 %collective-permute-start.10 = (f32[2,512,128]{2,1,0:T(8,128)S(1)}, f32[2,512,128]{2,1,0:T(8,128)S(1)}, u32[]{:S(2)}, u32[]{:S(2)}) collective-permute-start(f32[2,512,128]{2,1,0:T(8,128)S(1)} %slice.123), channel_id=1, source_target_pairs={{2,0},{3,1},{4,2},{5,3},{6,4},{7,5},{8,6},{9,7},{10,8},{11,9},{12,... | collective-permute-start | bytes 1572872 | tf_op jit(solution)/shard_map/ppermute | solution.py:14
  110.8 35.8 %collective-permute-start.9 = (f32[2,256,128]{2,1,0:T(8,128)S(1)}, f32[2,256,128]{2,1,0:T(8,128)S(1)}, u32[]{:S(2)}, u32[]{:S(2)}) collective-permute-start(f32[2,256,128]{2,1,0:T(8,128)S(1)} %slice.121), channel_id=1, source_target_pairs={{4,0},{5,1},{6,2},{7,3},{8,4},{9,5},{10,6},{11,7},{12,8},{13,9},{1... | collective-permute-start | bytes 786440 | tf_op jit(solution)/shard_map/ppermute | solution.py:14
  122.2 30.0 %collective-permute-start.17 = (f32[2,256,128]{2,1,0:T(8,128)S(1)}, f32[2,256,128]{2,1,0:T(8,128)S(1)}, u32[]{:S(2)}, u32[]{:S(2)}) collective-permute-start(f32[2,256,128]{2,1,0:T(8,128)S(1)} %get-tuple-element.433), channel_id=1, source_target_pairs={{256,0},{257,1},{258,2},{259,3},{260,4},{261,5},{262,6},{263,7},{2... | collective-permute-start | bytes 786440 | tf_op jit(solution)/shard_map/ppermute | solution.py:14
  123.5 42.0 %collective-permute-start.16 = (f32[2,256,128]{2,1,0:T(8,128)S(1)}, f32[2,256,128]{2,1,0:T(8,128)S(1)}, u32[]{:S(2)}, u32[]{:S(2)}) collective-permute-start(f32[2,256,128]{2,1,0:T(8,128)S(1)} %get-tuple-element.429), channel_id=1, source_target_pairs={{128,0},{129,1},{130,2},{131,3},{132,4},{133,5},{134,6},{135,7},{1... | collective-permute-start | bytes 786440 | tf_op jit(solution)/shard_map/ppermute | solution.py:14
  124.8 42.6 %collective-permute-start.15 = (f32[2,256,128]{2,1,0:T(8,128)S(1)}, f32[2,256,128]{2,1,0:T(8,128)S(1)}, u32[]{:S(2)}, u32[]{:S(2)}) collective-permute-start(f32[2,256,128]{2,1,0:T(8,128)S(1)} %get-tuple-element.430), channel_id=1, source_target_pairs={{64,0},{65,1},{66,2},{67,3},{68,4},{69,5},{70,6},{71,7},{72,8},{73... | collective-permute-start | bytes 786440 | tf_op jit(solution)/shard_map/ppermute | solution.py:14
  146.6 20.8 %collective-permute-start.14 = (f32[2,256,128]{2,1,0:T(8,128)S(1)}, f32[2,256,128]{2,1,0:T(8,128)S(1)}, u32[]{:S(2)}, u32[]{:S(2)}) collective-permute-start(f32[2,256,128]{2,1,0:T(8,128)S(1)} %get-tuple-element.431), channel_id=1, source_target_pairs={{32,0},{33,1},{34,2},{35,3},{36,4},{37,5},{38,6},{39,7},{40,8},{41... | collective-permute-start | bytes 786440 | tf_op jit(solution)/shard_map/ppermute | solution.py:14
  149.5 17.9 %collective-permute-start.13 = (f32[2,256,128]{2,1,0:T(8,128)S(1)}, f32[2,256,128]{2,1,0:T(8,128)S(1)}, u32[]{:S(2)}, u32[]{:S(2)}) collective-permute-start(f32[2,256,128]{2,1,0:T(8,128)S(1)} %get-tuple-element.432), channel_id=1, source_target_pairs={{16,0},{17,1},{18,2},{19,3},{20,4},{21,5},{22,6},{23,7},{24,8},{25... | collective-permute-start | bytes 786440 | tf_op jit(solution)/shard_map/ppermute | solution.py:14
  152.2 28.7 %collective-permute-start.12 = (f32[2,256,128]{2,1,0:T(8,128)S(1)}, f32[2,256,128]{2,1,0:T(8,128)S(1)}, u32[]{:S(2)}, u32[]{:S(2)}) collective-permute-start(f32[2,256,128]{2,1,0:T(8,128)S(1)} %get-tuple-element.428), channel_id=1, source_target_pairs={{8,0},{9,1},{10,2},{11,3},{12,4},{13,5},{14,6},{15,7},{16,8},{17,9... | collective-permute-start | bytes 786440 | tf_op jit(solution)/shard_map/ppermute | solution.py:14
  165.5 15.4 %collective-permute-start.11 = (f32[2,256,128]{2,1,0:T(8,128)S(1)}, f32[2,256,128]{2,1,0:T(8,128)S(1)}, u32[]{:S(2)}, u32[]{:S(2)}) collective-permute-start(f32[2,256,128]{2,1,0:T(8,128)S(1)} %slice.143), channel_id=1, source_target_pairs={{1,0},{2,1},{3,2},{4,3},{5,4},{6,5},{7,6},{8,7},{9,8},{10,9},{11,1... | collective-permute-start | bytes 786440 | tf_op jit(solution)/shard_map/ppermute | solution.py:14
where the time goes:
time: 183 us; the launch traced here: 182 us
  starting transfers between devices  77.4 us (42%)
  waiting for transfers between devices  41.8 us (23%)
  matrix products  34.4 us (19%)
  local copies, waits for them, and re-layouts  17.5 us (10%)
  other arithmetic  8.85 us (5%)
    ppermute x18, starting transfers between devices, shifted(): return lax.ppermute(value, axis, pairs)  77.4 us
    ppermute x18, waiting for transfers between devices, shifted(): return lax.ppermute(value, axis, pairs)  41.8 us
    dot_general x4, matrix products, sub_block(): jnp.einsum('rd,kd->rk', q_rows, key_rows, preferred_element_type=jnp.floa...  9.07 us
    squeeze x4, local copies, waits for them, and re-layouts, sub_block(): key_rows = jnp.concatenate([window_part[0], far_part[0]], axis=0)  7.21 us
    slice x4, local copies, waits for them, and re-layouts, sub_block(): key_rows = jnp.concatenate([window_part[0], far_part[0]], axis=0)  7.02 us
    dot_general x4, matrix products, sub_block(): jnp.einsum('rk,rd->kd', score_grad, q_rows, preferred_element_type=jnp.fl...  6.47 us
    dot_general x4, matrix products, sub_block(): jnp.dot(probs_low, value_rows, preferred_element_type=jnp.float32)  5.65 us
    dot_general x4, matrix products, sub_block(): jnp.dot(score_grad, key_rows, preferred_element_type=jnp.float32)  5.36 us
  transfers between devices with their start and end apart: 18, of which 5 were waited for; matrix products, arithmetic and copies ran while one was open for 1% of the time, Pallas kernels for 0%

commit v1 on v0

v1 whole, which is shorter than its diff:
```python
import functools

import jax
import jax.numpy as jnp
from jax import lax
from jax.experimental import pallas as pl
from jax.experimental.pallas import tpu as pltpu
from jax.sharding import PartitionSpec as P

BLK = 128
F32 = jnp.float32
BF16 = jnp.bfloat16
MESH = pl.DeviceIdType.MESH
NEG = -1e30
NT = (((1,), (1,)), ((), ()))
NN = (((1,), (0,)), ((), ()))

DISTS = (1, 2, 3, 4, 8, 16, 32, 64, 128, 256)
SLOT = {d: i for i, d in enumerate(DISTS)}
PAIRS = ((8, 16), (64, 32), (128, 256))
OWN = 4
GROUPS = 8


def dot(a, b, dims):
    return lax.dot_general(a, b, dims, preferred_element_type=F32)


def kernel(
    inner, total, q, do, k, v, out, dq, dk, dv,
    win, far, score, prob, top, inv, dlow, qt, dt, delta, term, got, own,
    fsend, frecv, bsend, brecv,
):
    me = lax.axis_index("ctxa") * inner + lax.axis_index("ctxb")
    core = (me // inner) % 2
    scale = 1.0 / BLK**0.5
    unit = scale * 1.4426950408889634

    def place(delta_):
        return ((me + delta_) // inner, (me + delta_) % inner)

    mate = inner * (1 - 2 * core)

    def exists(delta_):
        return (me + delta_ >= 0) & (me + delta_ < total)

    barrier = pltpu.get_barrier_semaphore()
    count = jnp.int32(1)
    pl.semaphore_signal(barrier, inc=1, device_id=place(mate), device_id_type=MESH)
    for step in (1, -1, 8, -8, 64, -64, 128, -128):
        ok = exists(step)

        @pl.when(ok)
        def _(step=step):
            pl.semaphore_signal(barrier, inc=1, device_id=place(step), device_id_type=MESH)

        count = count + ok.astype(jnp.int32)
    pl.semaphore_wait(barrier, count)

    def held(kind, dist):
        if dist == 0:
            return k if kind == 0 else v
        if dist <= 4:
            return win.at[kind, dist - 1]
        for i, pair in enumerate(PAIRS):
            if dist in pair:
                return far.at[kind, i, :, pair.index(dist)]

    forward = [
        (0, 64, 64), (0, 1, 1), (0, 8, 8), (64, 64, 128), (1, 1, 2), (8, 8, 16),
        (128, 128, 256), (2, 1, 3), (3, 1, 4), (0, 32, 32), (64, -32, 32),
    ]

    def forward_ok(item):
        source, step, _ = item
        ok = (me - source >= 0) & exists(step)
        if step == 32:
            ok = core == 0
        if step == -32:
            ok = ok & (core == 1)
        return ok

    def forward_copy(kind, i):
        source, step, target = forward[i]
        return pltpu.make_async_remote_copy(
            src_ref=held(kind, source),
            dst_ref=held(kind, target),
            send_sem=fsend.at[kind, i],
            recv_sem=frecv.at[kind, SLOT[target]],
            device_id=place(step),
            device_id_type=MESH,
        )

    def pass_on(kind, dist):
        for i, item in enumerate(forward):
            if item[0] == dist:

                @pl.when(forward_ok(item))
                def _(i=i):
                    forward_copy(kind, i).start()

    def arrive(kind, dist):
        i = [item[2] for item in forward].index(dist)

        @pl.when(me >= dist)
        def _():
            forward_copy(kind, i).wait_recv()

        pass_on(kind, dist)

    for kind in range(2):
        pass_on(kind, 0)

    for dist in DISTS:

        @pl.when(me < dist)
        def _(dist=dist):
            for kind in range(2):
                ref = held(kind, dist)
                ref[...] = jnp.zeros(ref.shape, BF16)

    def operand(kind, group, b):
        if group == OWN:
            value = (k if kind == 0 else v)[...]
        elif group < OWN:
            value = win[kind, group]
        else:
            value = far[kind, group - OWN - 1, b]
        return value.reshape(2 * BLK, BLK)

    def scores(group):
        def body(b, _):
            keys = operand(0, group, b)
            for c in range(4):
                rows = pl.ds(c * 256, 256)
                s = dot(q[b, rows, :], keys, NT)
                if group == OWN or group == 3:
                    tok = b * BLK + (c * 256 + lax.broadcasted_iota(jnp.int32, (256, 256), 0)) // 8
                    col = lax.broadcasted_iota(jnp.int32, (256, 256), 1)
                    seen = col <= tok if group == OWN else (col > tok) & (me >= 4)
                    s = jnp.where(seen, s, NEG)
                    s0, s1 = s[:, :BLK], s[:, BLK:]
                else:
                    pair = (group + 1,) * 2 if group < OWN else PAIRS[group - OWN - 1]
                    s0 = jnp.where(me >= pair[0], s[:, :BLK], NEG)
                    s1 = jnp.where(me >= pair[1], s[:, BLK:], NEG)
                score[b, group, rows, :BLK] = s0
                score[b, group, rows, BLK:] = s1
                most = jnp.maximum(s0, s1)
                if group != OWN:
                    most = jnp.maximum(most, top[b, rows, :])
                top[b, rows, :] = most
            return 0

        lax.fori_loop(0, 2, body, 0)

    for b in range(2):
        for c in range(8):
            qt[b, :, c * BLK : (c + 1) * BLK] = q[b, c * BLK : (c + 1) * BLK, :].T
    scores(OWN)
    for dist in (1, 8, 64):
        arrive(0, dist)
    scores(0)
    for dist in (1, 8, 64):
        arrive(1, dist)
    for dist in (2, 16, 128):
        arrive(0, dist)
    scores(1)
    scores(5)
    for dist in (2, 16, 128):
        arrive(1, dist)
    arrive(0, 3)
    scores(2)
    arrive(1, 3)
    arrive(0, 32)
    scores(6)
    arrive(0, 4)
    scores(3)
    arrive(0, 256)
    scores(7)

    def soften(i, _):
        b = i // 8
        start = pl.multiple_of((i % 8) * BLK, BLK)
        rows = pl.ds(start, BLK)
        most = jnp.max(top[b, rows, :], axis=1, keepdims=True) * unit
        most = jnp.broadcast_to(most, (BLK, BLK))
        sums = jnp.zeros((BLK, BLK), F32)
        for group in range(GROUPS):
            for h in range(2):
                lanes = slice(h * BLK, (h + 1) * BLK)
                e = jnp.exp2(score[b, group, rows, lanes] * unit - most)
                sums = sums + e
                prob[b, group, rows, lanes] = e.astype(BF16)
        part = jnp.broadcast_to(1.0 / jnp.sum(sums, axis=1, keepdims=True), (BLK, BLK))
        inv[b, rows, :] = part
        low = (do[b, rows, :].astype(F32) * part).astype(BF16)
        dlow[b, rows, :] = low
        dt[b, :, rows] = low.T
        return 0

    lax.fori_loop(0, 16, soften, 0)

    back = [
        (256, -128, ()), (4, -1, ()), (16, -8, ()), (128, -64, (256,)), (3, -1, (4,)),
        (8, -8, (16,)), (64, -64, (128, 32)), (2, -1, (3,)), (1, -1, (2,)), (32, 0, ()),
    ]
    back_index = {item[0]: i for i, item in enumerate(back)}
    back_step = {item[0]: -item[1] for item in back}

    def back_copy(kind, dist):
        i = back_index[dist]
        step = back[i][1] if dist != 32 else mate
        return pltpu.make_async_remote_copy(
            src_ref=term.at[kind, SLOT[dist]],
            dst_ref=got.at[kind, SLOT[dist]],
            send_sem=bsend.at[kind, i],
            recv_sem=brecv.at[kind, SLOT[dist]],
            device_id=place(step),
            device_id_type=MESH,
        )

    def send_back(kind, dist):
        mine = SLOT[dist]
        for other in back[back_index[dist]][2]:
            if other == 32:
                ok = (me >= dist) & (core == 1)
            else:
                ok = (me >= dist) & exists(back_step[other])

            @pl.when(ok)
            def _(other=other):
                back_copy(kind, other).wait_recv()
                term[kind, mine] = (
                    term[kind, mine].astype(F32) + got[kind, SLOT[other]].astype(F32)
                ).astype(BF16)

        @pl.when(me >= dist)
        def _():
            back_copy(kind, dist).start()

    def reduce_rows(kind, group, left, factor):
        if group <= OWN:
            r = dot(left[0], prob[0, group], NN) + dot(left[1], prob[1, group], NN)
            if group == OWN:
                own[kind] = r * factor
            else:
                term[kind, group] = (r * factor).astype(BF16)
        else:
            pair = PAIRS[group - OWN - 1]
            for b in range(2):
                r = (dot(left[b], prob[b, group], NN) * factor).astype(BF16)
                for h in range(2):
                    term[kind, SLOT[pair[h]], :, b * BLK : (b + 1) * BLK] = r[
                        :, h * BLK : (h + 1) * BLK
                    ]

    reduce_rows(1, 7, dt, 1.0)
    send_back(1, 256)
    reduce_rows(1, 3, dt, 1.0)
    send_back(1, 4)
    reduce_rows(1, 5, dt, 1.0)
    send_back(1, 16)
    reduce_rows(1, 6, dt, 1.0)
    send_back(1, 32)
    reduce_rows(1, 2, dt, 1.0)
    reduce_rows(1, 1, dt, 1.0)
    send_back(1, 3)
    reduce_rows(1, 0, dt, 1.0)
    reduce_rows(1, OWN, dt, 1.0)
    send_back(1, 128)
    send_back(1, 8)

    for dist in (32, 4, 256):
        arrive(1, dist)

    def attend(i, _):
        b = i // 4
        rows = pl.ds(pl.multiple_of((i % 4) * 256, 256), 256)
        acc = dot(prob[b, 0, rows, :], operand(1, 0, b), NN)
        for group in range(1, GROUPS):
            acc = acc + dot(prob[b, group, rows, :], operand(1, group, b), NN)
        low = (acc * inv[b, rows, :]).astype(BF16)
        out[b, rows, :] = low
        d = jnp.sum(dlow[b, rows, :].astype(F32) * low.astype(F32), axis=1, keepdims=True)
        delta[b, rows, :] = jnp.broadcast_to(d, (256, BLK))
        return 0

    lax.fori_loop(0, 8, attend, 0, unroll=2)
    send_back(1, 2)

    def score_grads(group):
        def body(b, _):
            values = operand(1, group, b)
            for c in range(4):
                rows = pl.ds(c * 256, 256)
                dp = dot(dlow[b, rows, :], values, NT)
                d = delta[b, rows, :]
                for h in range(2):
                    lanes = slice(h * BLK, (h + 1) * BLK)
                    p = prob[b, group, rows, lanes].astype(F32)
                    prob[b, group, rows, lanes] = (p * (dp[:, lanes] - d)).astype(BF16)
            return 0

        lax.fori_loop(0, 2, body, 0)
        reduce_rows(0, group, qt, scale)

    score_grads(7)
    send_back(0, 256)
    send_back(1, 64)
    score_grads(3)
    send_back(0, 4)
    send_back(1, 1)
    score_grads(5)
    send_back(0, 16)
    score_grads(6)
    send_back(0, 32)
    score_grads(2)
    send_back(0, 3)
    send_back(0, 128)
    score_grads(1)
    send_back(0, 2)
    send_back(0, 8)
    score_grads(0)
    send_back(0, 64)
    send_back(0, 1)
    score_grads(OWN)

    def query_grads(i, _):
        b = i // 4
        rows = pl.ds(pl.multiple_of((i % 4) * 256, 256), 256)
        acc = dot(prob[b, 0, rows, :], operand(0, 0, b), NN)
        for group in range(1, GROUPS):
            acc = acc + dot(prob[b, group, rows, :], operand(0, group, b), NN)
        dq[b, rows, :] = (acc * scale).astype(BF16)
        return 0

    lax.fori_loop(0, 8, query_grads, 0, unroll=2)

    for kind, result in ((1, dv), (0, dk)):
        for dist in (1, 8, 64, 32):
            ok = (core == 0) if dist == 32 else exists(dist)

            @pl.when(ok)
            def _(kind=kind, dist=dist):
                back_copy(kind, dist).wait_recv()
                own[kind] = own[kind] + got[kind, SLOT[dist]].astype(F32)

        result[...] = own[kind].T.astype(BF16)

    for kind in range(2):
        for i, item in enumerate(forward):

            @pl.when(forward_ok(item))
            def _(kind=kind, i=i):
                forward_copy(kind, i).wait_send()

        for dist in DISTS:

            @pl.when(me >= dist)
            def _(kind=kind, dist=dist):
                back_copy(kind, dist).wait_send()


def solution(mesh):
    inner = mesh.shape["ctxb"]
    total = mesh.shape["ctxa"] * inner

    def body(queries, key_vectors, value_vectors, out_grad):
        toks, heads, width = queries.shape
        rows = toks * heads // 2
        big = (2, rows, width)
        vmem = pl.BlockSpec(memory_space=pltpu.VMEM)
        attention, query_grad, key_grad, value_grad = pl.pallas_call(
            functools.partial(kernel, inner, total),
            out_shape=(
                jax.ShapeDtypeStruct(big, BF16),
                jax.ShapeDtypeStruct(big, BF16),
                jax.ShapeDtypeStruct((toks, width), BF16),
                jax.ShapeDtypeStruct((toks, width), BF16),
            ),
            in_specs=[vmem] * 4,
            out_specs=[vmem] * 4,
            scratch_shapes=[
                pltpu.VMEM((2, 4, 2, BLK, width), BF16),
                pltpu.VMEM((2, 3, 2, 2, BLK, width), BF16),
                pltpu.VMEM((2, GROUPS, rows, 2 * BLK), F32),
                pltpu.VMEM((2, GROUPS, rows, 2 * BLK), BF16),
                pltpu.VMEM(big, F32),
                pltpu.VMEM(big, F32),
                pltpu.VMEM(big, BF16),
                pltpu.VMEM((2, width, rows), BF16),
                pltpu.VMEM((2, width, rows), BF16),
                pltpu.VMEM(big, F32),
                pltpu.VMEM((2, 10, width, 2 * BLK), BF16),
                pltpu.VMEM((2, 10, width, 2 * BLK), BF16),
                pltpu.VMEM((2, width, 2 * BLK), F32),
                pltpu.SemaphoreType.DMA((2, 11)),
                pltpu.SemaphoreType.DMA((2, 10)),
                pltpu.SemaphoreType.DMA((2, 10)),
                pltpu.SemaphoreType.DMA((2, 10)),
            ],
            compiler_params=pltpu.CompilerParams(
                collective_id=0, has_side_effects=True, vmem_limit_bytes=56 * 2**20
            ),
        )(
            queries.reshape(big),
            out_grad.reshape(big),
            key_vectors.reshape(2, BLK, width),
            value_vectors.reshape(2, BLK, width),
        )
        return (
            attention.reshape(queries.shape),
            query_grad.reshape(queries.shape),
            key_grad,
            value_grad,
        )

    tokens = P(("ctxa", "ctxb"), None)
    rows = P(("ctxa", "ctxb"), None, None)
    return jax.shard_map(
        body,
        mesh=mesh,
        in_specs=(rows, tokens, tokens, rows),
        out_specs=(rows, rows, tokens, tokens),
        check_vma=False,
    )
```

time: 183 us -> 73.2 us (0.40)
  the two profiles are of different devices: /device:TPU:121 before, /device:TPU:10 now
where the time goes in v1:
time: 73.2 us; the launch traced here: 73 us
  Pallas kernels  68 us (93%)
  local copies, waits for them, and re-layouts  4.28 us (6%)
    pallas_call x1, Pallas kernels, body(): pl.pallas_call(functools.partial(kernel, inner, total), out_shape=(jax.Sh...  68 us
    unnamed x10, local copies, waits for them, and re-layouts  4.28 us

profile of v1, /device:TPU:10, one launch (start us, length us, event | category | flops | bytes accessed | tf_op | source)
XLA Modules:
  0.0 73.0 jit_solution(14061434185958608056)
XLA Ops:
  0.6 68.0 %shard_map.75 = (bf16[2,1024,128]{2,1,0:T(8,128)(2,1)}, bf16[2,1024,128]{2,1,0:T(8,128)(2,1)}, bf16[256,128]{1,0:T(8,128)(2,1)}, bf16[256,128]{1,0:T(8,128)(2,1)}) custom-call(bf16[2,1024,128]{2,1,0:T(8,128)(2,1)} %bitcast.6, bf16[2,1024,128]{2,1,0:T(8,128)(2,1)} %bitcast.7, bf16[2,128,128]{2,1,0:T(8,128)(2,1)} %bitcast.10, bf16[2,128,128]{2,1,0:T(8,128)(2,1)} %bitcast.11), custom_call_target="tpu_custom_call" | custom-call | tf_op jit(solution)/shard_map/pallas_call | solution.py:374
  68.7 0.0 copy-start
  68.7 1.9 %copy.12 = bf16[256,8,128]{2,1,0:T(8,128)(2,1)} copy(bf16[256,8,128]{2,1,0:T(8,128)(2,1)} %bitcast.9) | data formatting | bytes 1048576
  70.6 0.0 copy-done
  70.6 0.0 copy-start.2
  70.6 0.8 %copy.13 = bf16[256,8,128]{2,1,0:T(8,128)(2,1)} copy(bf16[256,8,128]{2,1,0:T(8,128)(2,1)S(1)} %bitcast.8) | data formatting | bytes 1048576
  71.4 0.1 copy-done.2
  71.5 0.0 copy-start.1
  71.5 0.6 copy.14
  72.1 0.2 copy-done.1
  72.3 0.6 copy.15
Async XLA Ops:
  68.7 1.9 %copy-start = (bf16[2,1024,128]{2,1,0:T(8,128)(2,1)S(1)}, bf16[2,1024,128]{2,1,0:T(8,128)(2,1)}, u32[]{:S(2)}) copy-start(bf16[2,1024,128]{2,1,0:T(8,128)(2,1)} %get-tuple-element.9) | copy-start | bytes 1572868
  70.6 0.9 %copy-start.2 = (bf16[256,128]{1,0:T(8,128)(2,1)S(1)}, bf16[256,128]{1,0:T(8,128)(2,1)}, u32[]{:S(2)}) copy-start(bf16[256,128]{1,0:T(8,128)(2,1)} %get-tuple-element.18) | copy-start | bytes 196612
  71.5 0.9 %copy-start.1 = (bf16[256,128]{1,0:T(8,128)(2,1)S(1)}, bf16[256,128]{1,0:T(8,128)(2,1)}, u32[]{:S(2)}) copy-start(bf16[256,128]{1,0:T(8,128)(2,1)} %get-tuple-element.19) | copy-start | bytes 196612

commit v2 on v1

--- a/solution.py
+++ b/solution.py
@@ -47,7 +47,7 @@
     barrier = pltpu.get_barrier_semaphore()
     count = jnp.int32(1)
     pl.semaphore_signal(barrier, inc=1, device_id=place(mate), device_id_type=MESH)
-    for step in (1, -1, 8, -8, 64, -64, 128, -128):
+    for step in (2, -2, 128, -128, 64, -64, 1, -1, 8, -8, 16, -16):
         ok = exists(step)
 
         @pl.when(ok)
@@ -67,8 +67,8 @@
                 return far.at[kind, i, :, pair.index(dist)]
 
     forward = [
-        (0, 64, 64), (0, 1, 1), (0, 8, 8), (64, 64, 128), (1, 1, 2), (8, 8, 16),
-        (128, 128, 256), (2, 1, 3), (3, 1, 4), (0, 32, 32), (64, -32, 32),
+        (0, 2, 2), (0, 128, 128), (0, 64, 64), (0, 1, 1), (0, 8, 8), (0, 16, 16), (0, 32, 32),
+        (2, 2, 4), (2, 1, 3), (128, 128, 256), (64, -32, 32),
     ]
 
     def forward_ok(item):
@@ -108,8 +108,7 @@
 
         pass_on(kind, dist)
 
-    for kind in range(2):
-        pass_on(kind, 0)
+    pass_on(0, 0)
 
     for dist in DISTS:
 
@@ -133,7 +132,7 @@
             keys = operand(0, group, b)
             for c in range(4):
                 rows = pl.ds(c * 256, 256)
-                s = dot(q[b, rows, :], keys, NT)
+                s = dot(q[b, rows, :], keys, NT) * unit
                 if group == OWN or group == 3:
                     tok = b * BLK + (c * 256 + lax.broadcasted_iota(jnp.int32, (256, 256), 0)) // 8
                     col = lax.broadcasted_iota(jnp.int32, (256, 256), 1)
@@ -158,20 +157,19 @@
         for c in range(8):
             qt[b, :, c * BLK : (c + 1) * BLK] = q[b, c * BLK : (c + 1) * BLK, :].T
     scores(OWN)
-    for dist in (1, 8, 64):
+    for dist in (2, 128, 64):
         arrive(0, dist)
+    pass_on(1, 0)
+    arrive(0, 1)
     scores(0)
-    for dist in (1, 8, 64):
-        arrive(1, dist)
-    for dist in (2, 16, 128):
+    scores(1)
+    for dist in (8, 16):
         arrive(0, dist)
-    scores(1)
     scores(5)
-    for dist in (2, 16, 128):
+    for dist in (2, 128, 64):
         arrive(1, dist)
     arrive(0, 3)
     scores(2)
-    arrive(1, 3)
     arrive(0, 32)
     scores(6)
     arrive(0, 4)
@@ -183,27 +181,28 @@
         b = i // 8
         start = pl.multiple_of((i % 8) * BLK, BLK)
         rows = pl.ds(start, BLK)
-        most = jnp.max(top[b, rows, :], axis=1, keepdims=True) * unit
+        most = jnp.max(top[b, rows, :], axis=1, keepdims=True)
         most = jnp.broadcast_to(most, (BLK, BLK))
-        sums = jnp.zeros((BLK, BLK), F32)
+        sums = [jnp.zeros((BLK, BLK), F32)] * 2
         for group in range(GROUPS):
             for h in range(2):
                 lanes = slice(h * BLK, (h + 1) * BLK)
-                e = jnp.exp2(score[b, group, rows, lanes] * unit - most)
-                sums = sums + e
+                e = jnp.exp2(score[b, group, rows, lanes] - most)
+                sums[h] = sums[h] + e
                 prob[b, group, rows, lanes] = e.astype(BF16)
-        part = jnp.broadcast_to(1.0 / jnp.sum(sums, axis=1, keepdims=True), (BLK, BLK))
+        part = 1.0 / jnp.sum(sums[0] + sums[1], axis=1, keepdims=True)
+        part = jnp.broadcast_to(part, (BLK, BLK))
         inv[b, rows, :] = part
         low = (do[b, rows, :].astype(F32) * part).astype(BF16)
         dlow[b, rows, :] = low
         dt[b, :, rows] = low.T
         return 0
 
-    lax.fori_loop(0, 16, soften, 0)
+    lax.fori_loop(0, 16, soften, 0, unroll=4)
 
     back = [
-        (256, -128, ()), (4, -1, ()), (16, -8, ()), (128, -64, (256,)), (3, -1, (4,)),
-        (8, -8, (16,)), (64, -64, (128, 32)), (2, -1, (3,)), (1, -1, (2,)), (32, 0, ()),
+        (4, -2, ()), (3, -1, ()), (256, -128, ()), (32, 0, ()), (16, -16, ()), (8, -8, ()),
+        (1, -1, ()), (2, -2, (4, 3)), (128, -128, (256,)), (64, -64, (32,)),
     ]
     back_index = {item[0]: i for i, item in enumerate(back)}
     back_step = {item[0]: -item[1] for item in back}
@@ -255,23 +254,14 @@
                         :, h * BLK : (h + 1) * BLK
                     ]
 
-    reduce_rows(1, 7, dt, 1.0)
-    send_back(1, 256)
-    reduce_rows(1, 3, dt, 1.0)
-    send_back(1, 4)
-    reduce_rows(1, 5, dt, 1.0)
-    send_back(1, 16)
-    reduce_rows(1, 6, dt, 1.0)
-    send_back(1, 32)
-    reduce_rows(1, 2, dt, 1.0)
-    reduce_rows(1, 1, dt, 1.0)
-    send_back(1, 3)
-    reduce_rows(1, 0, dt, 1.0)
-    reduce_rows(1, OWN, dt, 1.0)
-    send_back(1, 128)
-    send_back(1, 8)
-
-    for dist in (32, 4, 256):
+    order = (
+        (3, (4,)), (2, (3,)), (7, (256,)), (6, (32,)), (5, (16, 8)), (1, ()), (0, (1,)), (OWN, ()),
+    )
+    for group, dists in order:
+        reduce_rows(1, group, dt, 1.0)
+        for dist in dists:
+            send_back(1, dist)
+    for dist in (1, 8, 16, 3, 4, 32, 256):
         arrive(1, dist)
 
     def attend(i, _):
@@ -286,8 +276,9 @@
         delta[b, rows, :] = jnp.broadcast_to(d, (256, BLK))
         return 0
 
-    lax.fori_loop(0, 8, attend, 0, unroll=2)
-    send_back(1, 2)
+    lax.fori_loop(0, 8, attend, 0, unroll=4)
+    for dist in (2, 128, 64):
+        send_back(1, dist)
 
     def score_grads(group):
         def body(b, _):
@@ -305,26 +296,13 @@
         lax.fori_loop(0, 2, body, 0)
         reduce_rows(0, group, qt, scale)
 
-    score_grads(7)
-    send_back(0, 256)
-    send_back(1, 64)
-    score_grads(3)
-    send_back(0, 4)
-    send_back(1, 1)
-    score_grads(5)
-    send_back(0, 16)
-    score_grads(6)
-    send_back(0, 32)
-    score_grads(2)
-    send_back(0, 3)
-    send_back(0, 128)
-    score_grads(1)
-    send_back(0, 2)
-    send_back(0, 8)
-    score_grads(0)
-    send_back(0, 64)
-    send_back(0, 1)
-    score_grads(OWN)
+    for group, dists in order:
+        score_grads(group)
+        for dist in dists:
+            send_back(0, dist)
+        if group == 0:
+            for dist in (2, 128, 64):
+                send_back(0, dist)
 
     def query_grads(i, _):
         b = i // 4
@@ -335,10 +313,10 @@
         dq[b, rows, :] = (acc * scale).astype(BF16)
         return 0
 
-    lax.fori_loop(0, 8, query_grads, 0, unroll=2)
+    lax.fori_loop(0, 8, query_grads, 0, unroll=4)
 
     for kind, result in ((1, dv), (0, dk)):
-        for dist in (1, 8, 64, 32):
+        for dist in (1, 8, 16, 2, 128, 64, 32):
             ok = (core == 0) if dist == 32 else exists(dist)
 
             @pl.when(ok)
@@ -360,6 +338,14 @@
             @pl.when(me >= dist)
             def _(kind=kind, dist=dist):
                 back_copy(kind, dist).wait_send()
+
+
+def hand_over(*refs):
+    copies = [pltpu.make_async_copy(refs[i], refs[4 + i], refs[8].at[i]) for i in range(4)]
+    for copy in copies:
+        copy.start()
+    for copy in copies:
+        copy.wait()
 
 
 def solution(mesh):
@@ -371,14 +357,15 @@
         rows = toks * heads // 2
         big = (2, rows, width)
         vmem = pl.BlockSpec(memory_space=pltpu.VMEM)
-        attention, query_grad, key_grad, value_grad = pl.pallas_call(
+        shapes = (
+            jax.ShapeDtypeStruct(big, BF16),
+            jax.ShapeDtypeStruct(big, BF16),
+            jax.ShapeDtypeStruct((toks, width), BF16),
+            jax.ShapeDtypeStruct((toks, width), BF16),
+        )
+        results = pl.pallas_call(
             functools.partial(kernel, inner, total),
-            out_shape=(
-                jax.ShapeDtypeStruct(big, BF16),
-                jax.ShapeDtypeStruct(big, BF16),
-                jax.ShapeDtypeStruct((toks, width), BF16),
-                jax.ShapeDtypeStruct((toks, width), BF16),
-            ),
+            out_shape=shapes,
             in_specs=[vmem] * 4,
             out_specs=[vmem] * 4,
             scratch_shapes=[
@@ -409,6 +396,14 @@
             key_vectors.reshape(2, BLK, width),
             value_vectors.reshape(2, BLK, width),
         )
+        place = pl.BlockSpec(memory_space=pl.ANY)
+        attention, query_grad, key_grad, value_grad = pl.pallas_call(
+            hand_over,
+            out_shape=shapes,
+            in_specs=[place] * 4,
+            out_specs=[place] * 4,
+            scratch_shapes=[pltpu.SemaphoreType.DMA((4,))],
+        )(*results)
         return (
             attention.reshape(queries.shape),
             query_grad.reshape(queries.shape),

time: 73.2 us -> 98 us (1.34)
  the two profiles are of different devices: /device:TPU:10 before, /device:TPU:6 now
where the time goes in v2:
time: 98 us; the launch traced here: 97.8 us
  Pallas kernels  97.2 us (99%)
    pallas_call x1, Pallas kernels, body(): pl.pallas_call(functools.partial(kernel, inner, total), out_shape=shapes,...  60.3 us
    pallas_call x1, Pallas kernels, body(): pl.pallas_call(hand_over, out_shape=shapes, in_specs=[place] * 4, out_spe...  36.9 us

profile of v2, /device:TPU:6, one launch (start us, length us, event | category | flops | bytes accessed | tf_op | source)
XLA Modules:
  0.0 97.8 jit_solution(5430788075848381955)
XLA Ops:
  0.6 60.3 %shard_map.75 = (bf16[2,1024,128]{2,1,0:T(8,128)(2,1)}, bf16[2,1024,128]{2,1,0:T(8,128)(2,1)}, bf16[256,128]{1,0:T(8,128)(2,1)}, bf16[256,128]{1,0:T(8,128)(2,1)}) custom-call(bf16[2,1024,128]{2,1,0:T(8,128)(2,1)} %bitcast.6, bf16[2,1024,128]{2,1,0:T(8,128)(2,1)} %bitcast.7, bf16[2,128,128]{2,1,0:T(8,128)(2,1)} %bitcast.8, bf16[2,128,128]{2,1,0:T(8,128)(2,1)} %bitcast.9), custom_call_target="tpu_custom_call" | custom-call | tf_op jit(solution)/shard_map/pallas_call | solution.py:366
  60.9 36.9 %shard_map.76 = (bf16[2,1024,128]{2,1,0:T(8,128)(2,1)}, bf16[2,1024,128]{2,1,0:T(8,128)(2,1)}, bf16[256,128]{1,0:T(8,128)(2,1)}, bf16[256,128]{1,0:T(8,128)(2,1)}) custom-call(bf16[2,1024,128]{2,1,0:T(8,128)(2,1)} %get-tuple-element.12.refs_0_, bf16[2,1024,128]{2,1,0:T(8,128)(2,1)} %get-tuple-element.13.refs_1_, bf16[256,128]{1,0:T(8,128)(2,1)} %get-tuple-element.14.refs_2_, ...), custom_call_target="tpu_custom_call" | custom-call | tf_op jit(solution)/shard_map/pallas_call | solution.py:400

commit v3 on v2

--- a/solution.py
+++ b/solution.py
@@ -128,7 +128,7 @@
         return value.reshape(2 * BLK, BLK)
 
     def scores(group):
-        def body(b, _):
+        for b in range(2):
             keys = operand(0, group, b)
             for c in range(4):
                 rows = pl.ds(c * 256, 256)
@@ -149,9 +149,6 @@
                 if group != OWN:
                     most = jnp.maximum(most, top[b, rows, :])
                 top[b, rows, :] = most
-            return 0
-
-        lax.fori_loop(0, 2, body, 0)
 
     for b in range(2):
         for c in range(8):
@@ -201,8 +198,8 @@
     lax.fori_loop(0, 16, soften, 0, unroll=4)
 
     back = [
-        (4, -2, ()), (3, -1, ()), (256, -128, ()), (32, 0, ()), (16, -16, ()), (8, -8, ()),
-        (1, -1, ()), (2, -2, (4, 3)), (128, -128, (256,)), (64, -64, (32,)),
+        (4, -4, ()), (3, -1, ()), (256, -256, ()), (128, -128, ()), (32, 0, ()), (16, -16, ()),
+        (8, -8, ()), (1, -1, ()), (2, -2, (3,)), (64, -64, (32,)),
     ]
     back_index = {item[0]: i for i, item in enumerate(back)}
     back_step = {item[0]: -item[1] for item in back}
@@ -255,7 +252,8 @@
                     ]
 
     order = (
-        (3, (4,)), (2, (3,)), (7, (256,)), (6, (32,)), (5, (16, 8)), (1, ()), (0, (1,)), (OWN, ()),
+        (3, (4,)), (2, (3,)), (7, (256, 128)), (1, ()), (6, (32,)), (5, (16, 8)), (0, (1,)),
+        (OWN, ()),
     )
     for group, dists in order:
         reduce_rows(1, group, dt, 1.0)
@@ -277,11 +275,9 @@
         return 0
 
     lax.fori_loop(0, 8, attend, 0, unroll=4)
-    for dist in (2, 128, 64):
-        send_back(1, dist)
 
     def score_grads(group):
-        def body(b, _):
+        for b in range(2):
             values = operand(1, group, b)
             for c in range(4):
                 rows = pl.ds(c * 256, 256)
@@ -291,18 +287,19 @@
                     lanes = slice(h * BLK, (h + 1) * BLK)
                     p = prob[b, group, rows, lanes].astype(F32)
                     prob[b, group, rows, lanes] = (p * (dp[:, lanes] - d)).astype(BF16)
-            return 0
-
-        lax.fori_loop(0, 2, body, 0)
         reduce_rows(0, group, qt, scale)
 
     for group, dists in order:
         score_grads(group)
         for dist in dists:
             send_back(0, dist)
+        if group == 7:
+            send_back(1, 2)
+            send_back(1, 64)
+        if group == 5:
+            send_back(0, 2)
         if group == 0:
-            for dist in (2, 128, 64):
-                send_back(0, dist)
+            send_back(0, 64)
 
     def query_grads(i, _):
         b = i // 4
@@ -316,7 +313,7 @@
     lax.fori_loop(0, 8, query_grads, 0, unroll=4)
 
     for kind, result in ((1, dv), (0, dk)):
-        for dist in (1, 8, 16, 2, 128, 64, 32):
+        for dist in (4, 256, 128, 8, 16, 1, 2, 64, 32):
             ok = (core == 0) if dist == 32 else exists(dist)
 
             @pl.when(ok)
@@ -400,7 +397,7 @@
         attention, query_grad, key_grad, value_grad = pl.pallas_call(
             hand_over,
             out_shape=shapes,
-            in_specs=[place] * 4,
+            in_specs=[vmem] * 4,
             out_specs=[place] * 4,
             scratch_shapes=[pltpu.SemaphoreType.DMA((4,))],
         )(*results)

time: 98 us -> 58.1 us (0.59)
  the two profiles are of different devices: /device:TPU:6 before, /device:TPU:248 now
where the time goes in v3:
time: 58.1 us; the launch traced here: 57.9 us
  Pallas kernels  57.1 us (98%)
  between operations  0.8 us (1%)
    pallas_call x1, Pallas kernels, body(): pl.pallas_call(functools.partial(kernel, inner, total), out_shape=shapes,...  54.9 us
    pallas_call x1, Pallas kernels, body(): pl.pallas_call(hand_over, out_shape=shapes, in_specs=[vmem] * 4, out_spec...  2.24 us

profile of v3, /device:TPU:248, one launch (start us, length us, event | category | flops | bytes accessed | tf_op | source)
XLA Modules:
  0.0 57.9 jit_solution(5229478544422904593)
XLA Ops:
  0.6 54.9 %shard_map.75 = (bf16[2,1024,128]{2,1,0:T(8,128)(2,1)}, bf16[2,1024,128]{2,1,0:T(8,128)(2,1)}, bf16[256,128]{1,0:T(8,128)(2,1)}, bf16[256,128]{1,0:T(8,128)(2,1)}) custom-call(bf16[2,1024,128]{2,1,0:T(8,128)(2,1)} %bitcast.6, bf16[2,1024,128]{2,1,0:T(8,128)(2,1)} %bitcast.7, bf16[2,128,128]{2,1,0:T(8,128)(2,1)} %bitcast.8, bf16[2,128,128]{2,1,0:T(8,128)(2,1)} %bitcast.9), custom_call_target="tpu_custom_call" | custom-call | tf_op jit(solution)/shard_map/pallas_call | solution.py:363
  55.5 2.2 %shard_map.76 = (bf16[2,1024,128]{2,1,0:T(8,128)(2,1)}, bf16[2,1024,128]{2,1,0:T(8,128)(2,1)}, bf16[256,128]{1,0:T(8,128)(2,1)}, bf16[256,128]{1,0:T(8,128)(2,1)}) custom-call(bf16[2,1024,128]{2,1,0:T(8,128)(2,1)} %get-tuple-element.12.refs_0_, bf16[2,1024,128]{2,1,0:T(8,128)(2,1)} %get-tuple-element.13.refs_1_, bf16[256,128]{1,0:T(8,128)(2,1)} %get-tuple-element.14.refs_2_, ...), custom_call_target="tpu_custom_call" | custom-call | tf_op jit(solution)/shard_map/pallas_call | solution.py:397

commit v4 on v3

--- a/solution.py
+++ b/solution.py
@@ -27,9 +27,9 @@
 
 
 def kernel(
-    inner, total, q, do, k, v, out, dq, dk, dv,
-    win, far, score, prob, top, inv, dlow, qt, dt, delta, term, got, own,
-    fsend, frecv, bsend, brecv,
+    inner, total, q_in, do_in, k, v, out, dq, dk, dv,
+    q, do, win, far, score, prob, top, inv, dlow, qt, dt, delta, term, got, own,
+    load, fsend, frecv, bsend, brecv,
 ):
     me = lax.axis_index("ctxa") * inner + lax.axis_index("ctxb")
     core = (me // inner) % 2
@@ -55,24 +55,33 @@
             pl.semaphore_signal(barrier, inc=1, device_id=place(step), device_id_type=MESH)
 
         count = count + ok.astype(jnp.int32)
+    loads = [
+        pltpu.make_async_copy(q_in, q, load.at[0]),
+        pltpu.make_async_copy(do_in, do, load.at[1]),
+    ]
+    for copy in loads:
+        copy.start()
     pl.semaphore_wait(barrier, count)
 
-    def held(kind, dist):
+    def held(kind, dist, half=None):
         if dist == 0:
-            return k if kind == 0 else v
+            ref = k if kind == 0 else v
+            return ref if half is None else ref.at[half]
         if dist <= 4:
-            return win.at[kind, dist - 1]
+            return win.at[kind, dist - 1] if half is None else win.at[kind, dist - 1, half]
         for i, pair in enumerate(PAIRS):
             if dist in pair:
-                return far.at[kind, i, :, pair.index(dist)]
+                return far.at[kind, i, slice(None) if half is None else half, pair.index(dist)]
 
     forward = [
-        (0, 2, 2), (0, 128, 128), (0, 64, 64), (0, 1, 1), (0, 8, 8), (0, 16, 16), (0, 32, 32),
-        (2, 2, 4), (2, 1, 3), (128, 128, 256), (64, -32, 32),
+        (0, 2, 2, 0), (0, 128, 128, 0), (0, 2, 2, 1), (0, 128, 128, 1), (0, 64, 64, None),
+        (0, 1, 1, None), (0, 8, 8, None), (0, 16, 16, None), (0, 32, 32, None),
+        (2, 2, 4, 0), (2, 1, 3, 0), (128, 128, 256, 0), (2, 2, 4, 1), (2, 1, 3, 1),
+        (128, 128, 256, 1), (64, -32, 32, None),
     ]
 
     def forward_ok(item):
-        source, step, _ = item
+        source, step = item[:2]
         ok = (me - source >= 0) & exists(step)
         if step == 32:
             ok = core == 0
@@ -81,34 +90,35 @@
         return ok
 
     def forward_copy(kind, i):
-        source, step, target = forward[i]
+        source, step, target, half = forward[i]
         return pltpu.make_async_remote_copy(
-            src_ref=held(kind, source),
-            dst_ref=held(kind, target),
+            src_ref=held(kind, source, half),
+            dst_ref=held(kind, target, half),
             send_sem=fsend.at[kind, i],
-            recv_sem=frecv.at[kind, SLOT[target]],
+            recv_sem=frecv.at[kind, SLOT[target], half or 0],
             device_id=place(step),
             device_id_type=MESH,
         )
 
-    def pass_on(kind, dist):
+    def pass_on(kind, dist, halves):
         for i, item in enumerate(forward):
-            if item[0] == dist:
+            if item[0] == dist and item[3] in halves:
 
                 @pl.when(forward_ok(item))
                 def _(i=i):
                     forward_copy(kind, i).start()
 
-    def arrive(kind, dist):
-        i = [item[2] for item in forward].index(dist)
-
-        @pl.when(me >= dist)
-        def _():
-            forward_copy(kind, i).wait_recv()
-
-        pass_on(kind, dist)
-
-    pass_on(0, 0)
+    def arrive(kind, dist, halves=(None, 0, 1)):
+        for half in halves:
+            into = [i for i, item in enumerate(forward) if item[2:] == (dist, half)]
+            if into:
+                @pl.when(me >= dist)
+                def _(i=into[0]):
+                    forward_copy(kind, i).wait_recv()
+
+                pass_on(kind, dist, (half,))
+
+    pass_on(0, 0, (None, 0, 1))
 
     for dist in DISTS:
 
@@ -150,21 +160,26 @@
                     most = jnp.maximum(most, top[b, rows, :])
                 top[b, rows, :] = most
 
+    loads[0].wait()
     for b in range(2):
         for c in range(8):
             qt[b, :, c * BLK : (c + 1) * BLK] = q[b, c * BLK : (c + 1) * BLK, :].T
     scores(OWN)
-    for dist in (2, 128, 64):
-        arrive(0, dist)
-    pass_on(1, 0)
+    for half in (0, 1):
+        for dist in (2, 128):
+            arrive(0, dist, (half,))
+    arrive(0, 64)
+    pass_on(1, 0, (None, 0, 1))
     arrive(0, 1)
     scores(0)
     scores(1)
     for dist in (8, 16):
         arrive(0, dist)
     scores(5)
-    for dist in (2, 128, 64):
-        arrive(1, dist)
+    for half in (0, 1):
+        for dist in (2, 128):
+            arrive(1, dist, (half,))
+    arrive(1, 64)
     arrive(0, 3)
     scores(2)
     arrive(0, 32)
@@ -195,6 +210,7 @@
         dt[b, :, rows] = low.T
         return 0
 
+    loads[1].wait()
     lax.fori_loop(0, 16, soften, 0, unroll=4)
 
     back = [
@@ -354,6 +370,7 @@
         rows = toks * heads // 2
         big = (2, rows, width)
         vmem = pl.BlockSpec(memory_space=pltpu.VMEM)
+        place = pl.BlockSpec(memory_space=pl.ANY)
         shapes = (
             jax.ShapeDtypeStruct(big, BF16),
             jax.ShapeDtypeStruct(big, BF16),
@@ -363,9 +380,11 @@
         results = pl.pallas_call(
             functools.partial(kernel, inner, total),
             out_shape=shapes,
-            in_specs=[vmem] * 4,
+            in_specs=[place, place, vmem, vmem],
             out_specs=[vmem] * 4,
             scratch_shapes=[
+                pltpu.VMEM(big, BF16),
+                pltpu.VMEM(big, BF16),
                 pltpu.VMEM((2, 4, 2, BLK, width), BF16),
                 pltpu.VMEM((2, 3, 2, 2, BLK, width), BF16),
                 pltpu.VMEM((2, GROUPS, rows, 2 * BLK), F32),
@@ -379,8 +398,9 @@
                 pltpu.VMEM((2, 10, width, 2 * BLK), BF16),
                 pltpu.VMEM((2, 10, width, 2 * BLK), BF16),
                 pltpu.VMEM((2, width, 2 * BLK), F32),
-                pltpu.SemaphoreType.DMA((2, 11)),
-                pltpu.SemaphoreType.DMA((2, 10)),
+                pltpu.SemaphoreType.DMA((2,)),
+                pltpu.SemaphoreType.DMA((2, 16)),
+                pltpu.SemaphoreType.DMA((2, 10, 2)),
                 pltpu.SemaphoreType.DMA((2, 10)),
                 pltpu.SemaphoreType.DMA((2, 10)),
             ],
@@ -393,7 +413,6 @@
             key_vectors.reshape(2, BLK, width),
             value_vectors.reshape(2, BLK, width),
         )
-        place = pl.BlockSpec(memory_space=pl.ANY)
         attention, query_grad, key_grad, value_grad = pl.pallas_call(
             hand_over,
             out_shape=shapes,

time: 58.1 us -> 56.9 us (0.979)
  Pallas kernels: 57.1 us -> 55.9 us
    pallas_call x1, Pallas kernels: 54.9 us -> 53.7 us  [body(): pl.pallas_call(functools.partial(kernel, inner, total), out_shape=shapes,...]
where the time goes in v4:
time: 56.9 us; the launch traced here: 56.7 us
  Pallas kernels  55.9 us (98%)
  between operations  0.8 us (1%)
    pallas_call x1, Pallas kernels, body(): pl.pallas_call(functools.partial(kernel, inner, total), out_shape=shapes,...  53.7 us
    pallas_call x1, Pallas kernels, body(): pl.pallas_call(hand_over, out_shape=shapes, in_specs=[vmem] * 4, out_spec...  2.24 us

profile of v4, /device:TPU:248, one launch (start us, length us, event | category | flops | bytes accessed | tf_op | source)
XLA Modules:
  0.0 56.7 jit_solution(13809512482032441125)
XLA Ops:
  0.6 53.7 %shard_map.75 = (bf16[2,1024,128]{2,1,0:T(8,128)(2,1)}, bf16[2,1024,128]{2,1,0:T(8,128)(2,1)}, bf16[256,128]{1,0:T(8,128)(2,1)}, bf16[256,128]{1,0:T(8,128)(2,1)}) custom-call(bf16[2,1024,128]{2,1,0:T(8,128)(2,1)} %bitcast.6, bf16[2,1024,128]{2,1,0:T(8,128)(2,1)} %bitcast.7, bf16[2,128,128]{2,1,0:T(8,128)(2,1)} %bitcast.8, bf16[2,128,128]{2,1,0:T(8,128)(2,1)} %bitcast.9), custom_call_target="tpu_custom_call" | custom-call | tf_op jit(solution)/shard_map/pallas_call | solution.py:380
  54.3 2.2 %shard_map.76 = (bf16[2,1024,128]{2,1,0:T(8,128)(2,1)}, bf16[2,1024,128]{2,1,0:T(8,128)(2,1)}, bf16[256,128]{1,0:T(8,128)(2,1)}, bf16[256,128]{1,0:T(8,128)(2,1)}) custom-call(bf16[2,1024,128]{2,1,0:T(8,128)(2,1)} %get-tuple-element.12.refs_0_, bf16[2,1024,128]{2,1,0:T(8,128)(2,1)} %get-tuple-element.13.refs_1_, bf16[256,128]{1,0:T(8,128)(2,1)} %get-tuple-element.14.refs_2_, ...), custom_call_target="tpu_custom_call" | custom-call | tf_op jit(solution)/shard_map/pallas_call | solution.py:416

commit v5 on v4

--- a/solution.py
+++ b/solution.py
@@ -20,6 +20,7 @@
 PAIRS = ((8, 16), (64, 32), (128, 256))
 OWN = 4
 GROUPS = 8
+EARLY = (OWN, 0, 1, 5)
 
 
 def dot(a, b, dims):
@@ -28,7 +29,7 @@
 
 def kernel(
     inner, total, q_in, do_in, k, v, out, dq, dk, dv,
-    q, do, win, far, score, prob, top, inv, dlow, qt, dt, delta, term, got, own,
+    q, do, win, far, score, prob, top, first, sums, inv, dlow, qt, dt, delta, term, got, own,
     load, fsend, frecv, bsend, brecv,
 ):
     me = lax.axis_index("ctxa") * inner + lax.axis_index("ctxb")
@@ -136,6 +137,47 @@
         else:
             value = far[kind, group - OWN - 1, b]
         return value.reshape(2 * BLK, BLK)
+
+    def exponentials(b, rows, groups, most):
+        total_ = [jnp.zeros((BLK, BLK), F32)] * 2
+        for group in groups:
+            for h in range(2):
+                lanes = slice(h * BLK, (h + 1) * BLK)
+                e = jnp.exp2(score[b, group, rows, lanes] - most)
+                total_[h] = total_[h] + e
+                prob[b, group, rows, lanes] = e.astype(BF16)
+        return total_[0] + total_[1]
+
+    def row_max(b, rows):
+        most = jnp.max(top[b, rows, :], axis=1, keepdims=True)
+        return jnp.broadcast_to(most, (BLK, BLK))
+
+    def soften_early(i, _):
+        b = i // 8
+        rows = pl.ds(pl.multiple_of((i % 8) * BLK, BLK), BLK)
+        most = row_max(b, rows)
+        first[b, rows, :] = most
+        sums[b, rows, :] = exponentials(b, rows, EARLY, most)
+        return 0
+
+    def soften(i, _):
+        b = i // 8
+        rows = pl.ds(pl.multiple_of((i % 8) * BLK, BLK), BLK)
+        most = row_max(b, rows)
+        shrink = jnp.exp2(first[b, rows, :] - most)
+        late = [g for g in range(GROUPS) if g not in EARLY]
+        all_ = sums[b, rows, :] * shrink + exponentials(b, rows, late, most)
+        part = 1.0 / jnp.sum(all_, axis=1, keepdims=True)
+        part = jnp.broadcast_to(part, (BLK, BLK))
+        for part_set, weight in enumerate((part * shrink, part)):
+            inv[part_set, b, rows, :] = weight
+            low = (do[b, rows, :].astype(F32) * weight).astype(BF16)
+            dlow[part_set, b, rows, :] = low
+            dt[part_set, b, :, rows] = low.T
+        return 0
+
+    def set_of(group):
+        return 0 if group in EARLY else 1
 
     def scores(group):
         for b in range(2):
@@ -176,6 +218,7 @@
     for dist in (8, 16):
         arrive(0, dist)
     scores(5)
+    lax.fori_loop(0, 16, soften_early, 0, unroll=4)
     for half in (0, 1):
         for dist in (2, 128):
             arrive(1, dist, (half,))
@@ -188,27 +231,6 @@
     scores(3)
     arrive(0, 256)
     scores(7)
-
-    def soften(i, _):
-        b = i // 8
-        start = pl.multiple_of((i % 8) * BLK, BLK)
-        rows = pl.ds(start, BLK)
-        most = jnp.max(top[b, rows, :], axis=1, keepdims=True)
-        most = jnp.broadcast_to(most, (BLK, BLK))
-        sums = [jnp.zeros((BLK, BLK), F32)] * 2
-        for group in range(GROUPS):
-            for h in range(2):
-                lanes = slice(h * BLK, (h + 1) * BLK)
-                e = jnp.exp2(score[b, group, rows, lanes] - most)
-                sums[h] = sums[h] + e
-                prob[b, group, rows, lanes] = e.astype(BF16)
-        part = 1.0 / jnp.sum(sums[0] + sums[1], axis=1, keepdims=True)
-        part = jnp.broadcast_to(part, (BLK, BLK))
-        inv[b, rows, :] = part
-        low = (do[b, rows, :].astype(F32) * part).astype(BF16)
-        dlow[b, rows, :] = low
-        dt[b, :, rows] = low.T
-        return 0
 
     loads[1].wait()
     lax.fori_loop(0, 16, soften, 0, unroll=4)
@@ -272,7 +294,7 @@
         (OWN, ()),
     )
     for group, dists in order:
-        reduce_rows(1, group, dt, 1.0)
+        reduce_rows(1, group, dt.at[set_of(group)], 1.0)
         for dist in dists:
             send_back(1, dist)
     for dist in (1, 8, 16, 3, 4, 32, 256):
@@ -281,13 +303,17 @@
     def attend(i, _):
         b = i // 4
         rows = pl.ds(pl.multiple_of((i % 4) * 256, 256), 256)
-        acc = dot(prob[b, 0, rows, :], operand(1, 0, b), NN)
-        for group in range(1, GROUPS):
-            acc = acc + dot(prob[b, group, rows, :], operand(1, group, b), NN)
-        low = (acc * inv[b, rows, :]).astype(BF16)
+        acc = [None, None]
+        for group in range(GROUPS):
+            r = dot(prob[b, group, rows, :], operand(1, group, b), NN)
+            n = set_of(group)
+            acc[n] = r if acc[n] is None else acc[n] + r
+        low = (acc[0] * inv[0, b, rows, :] + acc[1] * inv[1, b, rows, :]).astype(BF16)
         out[b, rows, :] = low
-        d = jnp.sum(dlow[b, rows, :].astype(F32) * low.astype(F32), axis=1, keepdims=True)
-        delta[b, rows, :] = jnp.broadcast_to(d, (256, BLK))
+        for n in range(2):
+            d = dlow[n, b, rows, :].astype(F32) * low.astype(F32)
+            d = jnp.sum(d, axis=1, keepdims=True)
+            delta[n, b, rows, :] = jnp.broadcast_to(d, (256, BLK))
         return 0
 
     lax.fori_loop(0, 8, attend, 0, unroll=4)
@@ -297,8 +323,8 @@
             values = operand(1, group, b)
             for c in range(4):
                 rows = pl.ds(c * 256, 256)
-                dp = dot(dlow[b, rows, :], values, NT)
-                d = delta[b, rows, :]
+                dp = dot(dlow[set_of(group), b, rows, :], values, NT)
+                d = delta[set_of(group), b, rows, :]
                 for h in range(2):
                     lanes = slice(h * BLK, (h + 1) * BLK)
                     p = prob[b, group, rows, lanes].astype(F32)
@@ -391,10 +417,12 @@
                 pltpu.VMEM((2, GROUPS, rows, 2 * BLK), BF16),
                 pltpu.VMEM(big, F32),
                 pltpu.VMEM(big, F32),
-                pltpu.VMEM(big, BF16),
+                pltpu.VMEM(big, F32),
+                pltpu.VMEM((2, *big), F32),
+                pltpu.VMEM((2, *big), BF16),
                 pltpu.VMEM((2, width, rows), BF16),
-                pltpu.VMEM((2, width, rows), BF16),
-                pltpu.VMEM(big, F32),
+                pltpu.VMEM((2, 2, width, rows), BF16),
+                pltpu.VMEM((2, *big), F32),
                 pltpu.VMEM((2, 10, width, 2 * BLK), BF16),
                 pltpu.VMEM((2, 10, width, 2 * BLK), BF16),
                 pltpu.VMEM((2, width, 2 * BLK), F32),

time: 56.9 us -> 56 us (0.984)
  Pallas kernels: 55.9 us -> 55 us
    pallas_call x1, Pallas kernels: 53.7 us -> 52.8 us  [body(): pl.pallas_call(functools.partial(kernel, inner, total), out_shape=shapes,...]
where the time goes in v5:
time: 56 us; the launch traced here: 55.8 us
  Pallas kernels  55 us (98%)
  between operations  0.8 us (1%)
    pallas_call x1, Pallas kernels, body(): pl.pallas_call(functools.partial(kernel, inner, total), out_shape=shapes,...  52.8 us
    pallas_call x1, Pallas kernels, body(): pl.pallas_call(hand_over, out_shape=shapes, in_specs=[vmem] * 4, out_spec...  2.24 us

profile of v5, /device:TPU:248, one launch (start us, length us, event | category | flops | bytes accessed | tf_op | source)
XLA Modules:
  0.0 55.8 jit_solution(13320440843234155441)
XLA Ops:
  0.6 52.8 %shard_map.75 = (bf16[2,1024,128]{2,1,0:T(8,128)(2,1)}, bf16[2,1024,128]{2,1,0:T(8,128)(2,1)}, bf16[256,128]{1,0:T(8,128)(2,1)}, bf16[256,128]{1,0:T(8,128)(2,1)}) custom-call(bf16[2,1024,128]{2,1,0:T(8,128)(2,1)} %bitcast.6, bf16[2,1024,128]{2,1,0:T(8,128)(2,1)} %bitcast.7, bf16[2,128,128]{2,1,0:T(8,128)(2,1)} %bitcast.8, bf16[2,128,128]{2,1,0:T(8,128)(2,1)} %bitcast.9), custom_call_target="tpu_custom_call" | custom-call | tf_op jit(solution)/shard_map/pallas_call | solution.py:406
  53.4 2.2 %shard_map.76 = (bf16[2,1024,128]{2,1,0:T(8,128)(2,1)}, bf16[2,1024,128]{2,1,0:T(8,128)(2,1)}, bf16[256,128]{1,0:T(8,128)(2,1)}, bf16[256,128]{1,0:T(8,128)(2,1)}) custom-call(bf16[2,1024,128]{2,1,0:T(8,128)(2,1)} %get-tuple-element.12.refs_0_, bf16[2,1024,128]{2,1,0:T(8,128)(2,1)} %get-tuple-element.13.refs_1_, bf16[256,128]{1,0:T(8,128)(2,1)} %get-tuple-element.14.refs_2_, ...), custom_call_target="tpu_custom_call" | custom-call | tf_op jit(solution)/shard_map/pallas_call | solution.py:444
